TPU v7x, 32 devices: a whole 2x2x4 slice. The times are simulated.
32 devices in a mesh: cfg: 2 (over y), row: 8 (over z, x), col: 2 (over core).
Axes of the slice: x: 2, y: 2, z: 4, core: 2. Of those that a mesh axis runs over, the one named last changes fastest.
Arguments:
- root_inv: bfloat16 [5120, 2560], P(('cfg', 'row'), 'col'), parts along dimension 0, as said below
- child_off: bfloat16 [2560, 65536], P('col', ('cfg', 'row')), parts along dimension 1, may hold values from -0.15625 to 0.15625
- child_inv: bfloat16 [4096, 65536], P('col', ('cfg', 'row')), parts along dimension 1, as said below
- struct: int32 [16, 5], P('cfg'), parts along dimension 0, may hold values from 0 to 9, as said below
Outputs:
- cross_cov: float32 [2560, 65536], P('col', ('cfg', 'row')), parts along dimension 1
- root_var: float32 [5120], P(('cfg', 'col')), parts along dimension 0
- child_var: float32 [65536], P(('cfg', 'row')), parts along dimension 0
There are 2 independent parts, one for each index of `cfg`. A program takes and returns all parts, laid end to end along the dimension named above; each array names one. Nothing has to cross between parts.
Inputs may be any that keep to these rules, and one draw needn't show every extreme that they name: `struct`: row c lists the 256-row tiles of the root in which supernode c's block of L has nonzeros, all distinct; rows 2q and 2q + 1 together list every tile once. `root_inv`: lower triangular. `child_inv`: each block of 4096 columns is lower triangular.
All inputs are finite; a program needn't handle non-finite values.
Results may differ from a plain program's by a relative error of at most 0.0027.
Values may be sent and summed in bfloat16 or wider, within the bound.
A program may use at most 256 MiB of HBM per device.

v0:
```python
import jax
import jax.numpy as jnp
from jax import lax
from jax.sharding import PartitionSpec as P

W1 = 4096
TILE = 256


def member_mask(struct, row_ids, col_ids):
    tile_ids = row_ids // TILE
    tile_hits = jnp.any(tile_ids[:, None, None] == struct[None, :, :], axis=2).astype(jnp.float32)
    owners = col_ids // W1
    groups = jnp.arange(struct.shape[0], dtype=jnp.int32)
    choose = (owners[None, :] == groups[:, None]).astype(jnp.float32)
    return (
        jnp.dot(
            tile_hits, choose, precision=lax.Precision.HIGHEST, preferred_element_type=jnp.float32
        )
        > 0.5
    )


def contract_rows(own_cols, product_rows):
    return lax.dot_general(
        own_cols, product_rows, (((0,), (0,)), ((), ())), preferred_element_type=jnp.float32
    )


def body(root_inv, child_off, child_inv, struct):
    half_cols = root_inv.shape[1]
    col_count = child_off.shape[1]
    half_start = lax.axis_index("col") * half_cols
    col_start = lax.axis_index("row") * col_count
    row_ids = half_start + jnp.arange(half_cols, dtype=jnp.int32)
    col_ids = col_start + jnp.arange(col_count, dtype=jnp.int32)
    member = member_mask(struct, row_ids, col_ids)
    masked_off = jnp.where(member, child_off, jnp.zeros_like(child_off))
    root_var = lax.psum(jnp.sum(jnp.square(root_inv.astype(jnp.float32)), axis=0), "row")
    empty = (jnp.zeros((half_cols, col_count), jnp.float32), jnp.zeros((half_cols,), jnp.float32))
    first_terms = jnp.dot(
        lax.all_gather(root_inv, "row", axis=0, tiled=True),
        masked_off,
        preferred_element_type=jnp.float32,
    )
    product = lax.psum(first_terms, "col").astype(jnp.bfloat16)
    totals = (contract_rows(lax.all_gather(root_inv, "row", axis=0, tiled=True), product), empty[1])
    cross_cov = jnp.where(member, -totals[0], jnp.zeros_like(totals[0]))
    local_terms = jnp.sum(jnp.square(child_inv.astype(jnp.float32)), axis=0) - jnp.sum(
        masked_off.astype(jnp.float32) * cross_cov, axis=0
    )
    child_var = lax.psum(local_terms, "col")
    return (cross_cov, root_var, child_var)


def solution(mesh):
    placed = (
        P(("cfg", "row"), "col"),
        P("col", ("cfg", "row")),
        P("col", ("cfg", "row")),
        P("cfg", None),
    )
    return jax.shard_map(
        body,
        mesh=mesh,
        in_specs=placed,
        out_specs=(P("col", ("cfg", "row")), P(("cfg", "col")), P(("cfg", "row"))),
        check_vma=False,
    )
```

profile of v0, /device:TPU:0, one launch (start us, length us, event | category | flops | bytes accessed | tf_op | source)
XLA Modules:
  0.0 314.6 jit_solution(3605254461940612151)
XLA Ops:
  7.2 0.0 all-gather.2.cloned.1.call-start
  7.2 0.7 all-gather.2.cloned.1.call-update
  7.9 0.8 copy.7
  8.7 1.3 multiply_reduce_fusion.2
  10.0 24.5 %psum.22 = f32[1280]{0:T(1024)} all-reduce(f32[1280]{0:T(1024)S(1)} %multiply_reduce_fusion.2), channel_id=1, replica_groups=mesh['cfg'=2,'row'=8,'col'=2] {'row'}, use_global_device_ids=true, to_apply=%region_3.4 | all-reduce | flops 1280 | bytes 10240 | tf_op jit(solution)/shard_map/psum | solution.py:39
  34.5 0.0 slice-start
  34.5 0.1 compare_reduce_fusion
  34.6 0.0 slice-start.1
  34.7 0.0 slice-start.2
  34.7 0.0 slice-start.3
  34.7 4.8 %convolution_compare_fusion = pred[1280,4096]{1,0:T(32,128)(4,1)} fusion(pred[1280,8]{0,1:T(8,128)(4,1)S(1)} %compare_reduce_fusion, s32[4096]{0:T(1024)S(1)} %add_select_fusion), kind=kOutput, calls=%fused_computation.6 | convolution fusion | flops 89161728 | bytes 5269504 | tf_op jit(solution)/shard_map/dot_general | solution.py:17
  39.5 0.0 slice-done
  39.5 0.0 slice-done.1
  39.5 1.7 slice-done.2
  41.2 1.2 slice-done.3
  42.4 4.1 %multiply_reduce_fusion = f32[4096]{0:T(1024)S(1)} fusion(bf16[2048,4096]{1,0:T(8,128)(2,1)S(1)} %bitcast.9), kind=kLoop, calls=%fused_computation | loop fusion | flops 25161728 | bytes 16793600 | tf_op jit(solution)/shard_map/reduce_sum | solution.py:49
  46.5 69.0 %all-gather.2.cloned.1.call-done = bf16[2560,1280]{1,0:T(8,128)(2,1)} async-done(((bf16[320,1280]{1,0:T(8,128)(2,1)}), bf16[2560,1280]{1,0:T(8,128)(2,1)}) %all-gather.2.cloned.1.call-update) | async-done | bytes 6553616 | tf_op jit(solution)/shard_map/all_gather | solution.py:47
  115.5 35.9 %convolution_bitcast_fusion = f32[2560,4096]{0,1:T(8,128)} fusion(bf16[2560,1280]{1,0:T(8,128)(2,1)} %all-gather.2.cloned.1.call-done, pred[1280,4096]{1,0:T(32,128)(4,1)} %convolution_compare_fusion, bf16[1280,4096]{1,0:T(8,128)(2,1)} %param.5), kind=kOutput, calls=%fused_computation.1 | convolution fusion | flops 26848788480 | bytes 64225280 | tf_op jit(solution)/shard_map/dot_general | solution.py:41
  151.4 111.0 %all-reduce.1 = bf16[2560,4096]{0,1:T(8,128)(2,1)} all-reduce(f32[2560,4096]{0,1:T(8,128)} %convolution_bitcast_fusion), channel_id=1, replica_groups=mesh['cfg'=2,'row'=8,'col'=2] {'col'}, use_global_device_ids=true, to_apply=%region_1.2 | all-reduce | flops 10485760 | bytes 62914560 | tf_op jit(solution)/shard_map/psum | solution.py:46
  262.4 41.2 %multiply_reduce_fusion.1 = (f32[4096]{0:T(1024)S(1)}, f32[1280,4096]{1,0:T(8,128)}) fusion(pred[1280,4096]{1,0:T(32,128)(4,1)} %convolution_compare_fusion, bf16[1280,4096]{1,0:T(8,128)(2,1)} %param.5, bf16[2560,4096]{0,1:T(8,128)(2,1)} %all-reduce.1, bf16[2560,1280]{1,0:T(8,128)(2,1)} %all-gather.2.cloned.1.call-done), kind=kOutput, calls=%fused_computation.3 | convolution fusion | flops 26874998784 | bytes 64241664 | tf_op jit(solution)/shard_map/dot_general | solution.py:25
  303.7 4.1 %psum.23 = f32[4096]{0:T(1024)} all-reduce(f32[4096]{0:T(1024)S(1)} %sub.17), channel_id=1, replica_groups=mesh['cfg'=2,'row'=8,'col'=2] {'col'}, use_global_device_ids=true, to_apply=%region_6.7 | all-reduce | flops 4096 | bytes 32768 | tf_op jit(solution)/shard_map/psum | solution.py:52
  (4 shorter events, 0.0 us)
Async XLA Ops:
  7.2 108.3 %all-gather.2.cloned.1.call-start = ((), (), s32[]{:S(2)}) async-start(), calls=%async_computation | async-start | bytes 7372800 | tf_op jit(solution)/shard_map/all_gather | solution.py:47
  34.5 5.0 %slice-start = ((s8[16777216]{0:T(1024)(128)(4,1)}), s8[4194304]{0:T(1024)(128)(4,1)S(1)}, s32[]{:S(2)}) async-start(s8[16777216]{0:T(1024)(128)(4,1)} %bitcast.8), calls=%async_computation.1 | async-start | bytes 8388608
  34.6 4.8 %slice-start.1 = ((s8[16777216]{0:T(1024)(128)(4,1)}), s8[4194304]{0:T(1024)(128)(4,1)S(1)}, s32[]{:S(2)}) async-start(s8[16777216]{0:T(1024)(128)(4,1)} %bitcast.8), calls=%async_computation.2 | async-start | bytes 8388608
  34.7 6.5 %slice-start.2 = ((s8[16777216]{0:T(1024)(128)(4,1)}), s8[4194304]{0:T(1024)(128)(4,1)S(1)}, s32[]{:S(2)}) async-start(s8[16777216]{0:T(1024)(128)(4,1)} %bitcast.8), calls=%async_computation.3 | async-start | bytes 8388608
  34.7 7.7 %slice-start.3 = ((s8[16777216]{0:T(1024)(128)(4,1)}), s8[4194304]{0:T(1024)(128)(4,1)S(1)}, s32[]{:S(2)}) async-start(s8[16777216]{0:T(1024)(128)(4,1)} %bitcast.8), calls=%async_computation.4 | async-start | bytes 8388608
Sparse Core Ops, SparseCore 0:
  10.2 105.2 all-gather.1
where the time goes:
time: 315 us
  blocking collectives  140 us (44%)
  matrix products  82 us (26%)
  waiting for transfers between devices  69.6 us (22%)
  between operations  14.1 us (4%)
  other arithmetic  5.58 us (2%)
  local copies, waits for them, and re-layouts  3.7 us (1%)
    psum x1, blocking collectives, body(): product = lax.psum(first_terms, 'col').astype(jnp.bfloat16)  111 us
    all_gather x1, waiting for transfers between devices, body(): lax.all_gather(root_inv, 'row', axis=0, tiled=True)  69 us
    dot_general x1, matrix products, contract_rows(): lax.dot_general(own_cols, product_rows, (((0,), (0,)), ((), ())), preferr...  41.2 us
    dot_general x1, matrix products, body(): jnp.dot(lax.all_gather(root_inv, 'row', axis=0, tiled=True), masked_off,...  35.9 us
    psum x1, blocking collectives, body(): lax.psum(jnp.sum(jnp.square(root_inv.astype(jnp.float32)), axis=0), 'row')  24.5 us
  transfers between devices with their start and end apart: 1, of which 1 were waited for; matrix products, arithmetic and copies ran while one was open for 4% of the time, Pallas kernels for 0%

commit v1 on v0

--- a/solution.py
+++ b/solution.py
@@ -1,6 +1,10 @@
+import functools
+
 import jax
 import jax.numpy as jnp
 from jax import lax
+from jax.experimental import pallas as pl
+from jax.experimental.pallas import tpu as pltpu
 from jax.sharding import PartitionSpec as P
 
 W1 = 4096
@@ -27,7 +31,7 @@
     )
 
 
-def body(root_inv, child_off, child_inv, struct):
+def plain_body(root_inv, child_off, child_inv, struct):
     half_cols = root_inv.shape[1]
     col_count = child_off.shape[1]
     half_start = lax.axis_index("col") * half_cols
@@ -53,6 +57,336 @@
     return (cross_cov, root_var, child_var)
 
 
+MESH = pl.DeviceIdType.MESH
+CHUNK = 512
+LAG = 1
+
+
+def gather_kernel(
+    inv_ref, off_ref, mask_ref, r_out, p_out, var_out,
+    r_buf, r_low, x_own, x_low, p_buf, r_masked, low_masked,
+    recv_sem, send_sem, low_sem, x_sem, x_recv, p_send, p_recv, p_local, r_local, own_sem,
+):
+    rows, half = inv_ref.shape
+    cols = off_ref.shape[1]
+    row = lax.axis_index("row")
+    core = lax.axis_index("col")
+    z, x = row // 2, row % 2
+    other = {"row": row, "col": 1 - core}
+    across = {"row": 2 * z + 1 - x}
+    below = {"row": lax.rem(row + 6, 8)}
+    above = {"row": lax.rem(row + 2, 8)}
+    widths = [min(half, -(-(k + 1) * rows // TILE) * TILE) for k in range(4)]
+
+    barrier = pltpu.get_barrier_semaphore()
+    pl.semaphore_signal(barrier, inc=1, device_id=across, device_id_type=MESH)
+    pl.semaphore_signal(barrier, inc=1, device_id={"col": 1 - core}, device_id_type=MESH)
+
+    @pl.when(z > 0)
+    def _():
+        pl.semaphore_signal(barrier, inc=1, device_id=below, device_id_type=MESH)
+
+    @pl.when(z < 3)
+    def _():
+        pl.semaphore_signal(barrier, inc=1, device_id=above, device_id_type=MESH)
+
+    own_copy = pltpu.make_async_copy(inv_ref, r_buf.at[row], own_sem)
+    own_copy.start()
+    x_copy = pltpu.make_async_copy(off_ref, x_own, x_sem.at[0])
+    x_copy.start()
+    pl.semaphore_wait(barrier, 3 + ((z + 1) // 2) % 2)
+
+    send_x = pltpu.make_async_remote_copy(
+        src_ref=off_ref, dst_ref=x_low, send_sem=x_sem.at[1], recv_sem=x_recv,
+        device_id={"col": 1 - core}, device_id_type=MESH,
+    )
+
+    def block_at(step):
+        s, flip = step // 2, step % 2
+        first, second = 1 + z % 2, 2 * (1 - z % 2) + z // 2
+        third = 3 * (1 - z // 2)
+        zb = z + ((s + 3) // 4) * (first - z) + (s // 2) * (second - first) + (s // 3) * (third - second)
+        return zb, flip, 2 * zb + (x + flip) % 2
+
+    def by_width(block, act):
+        depth = block - 4 * core
+        for k in range(4):
+            @pl.when((depth == k) if k < 3 else (depth >= 3))
+            def _(k=k):
+                act(widths[k])
+
+    def send(block, width, way, device):
+        view = r_buf.at[block, :, pl.ds(0, width)]
+        return pltpu.make_async_remote_copy(
+            src_ref=view, dst_ref=view, send_sem=send_sem.at[block, way], recv_sem=recv_sem.at[block],
+            device_id=device, device_id_type=MESH,
+        )
+
+    def send_low(block):
+        return pltpu.make_async_remote_copy(
+            src_ref=r_buf.at[block], dst_ref=r_low.at[block - 4],
+            send_sem=send_sem.at[block, 3], recv_sem=low_sem.at[block - 4],
+            device_id={"col": 1 - core}, device_id_type=MESH,
+        )
+
+    def keep(block, width):
+        return pltpu.make_async_copy(
+            r_buf.at[block, :, pl.ds(0, width)],
+            r_out.at[pl.ds(block * rows, rows), pl.ds(0, width)],
+            r_local.at[block],
+        )
+
+    def keep_p(block, slot):
+        return pltpu.make_async_copy(
+            p_buf.at[slot], p_out.at[pl.ds(block * rows, rows), :], p_local.at[slot]
+        )
+
+    def send_p(block, slot):
+        return pltpu.make_async_remote_copy(
+            src_ref=p_buf.at[slot], dst_ref=p_out.at[pl.ds(block * rows, rows), :],
+            send_sem=p_send.at[slot], recv_sem=p_recv.at[slot],
+            device_id={"col": 1 - core}, device_id_type=MESH,
+        )
+
+    def each_send(step, act):
+        zb, flip, block = block_at(step)
+
+        def routes(width):
+            @pl.when((flip == 0) & (zb >= z) & (z > 0))
+            def _():
+                act(send(block, width, 0, below))
+
+            @pl.when((flip == 0) & (zb <= z) & (z < 3))
+            def _():
+                act(send(block, width, 1, above))
+
+            @pl.when(flip == 0)
+            def _():
+                act(send(block, width, 2, across))
+
+        by_width(block, routes)
+
+        @pl.when((core == 0) & (block >= 4))
+        def _():
+            act(send_low(block))
+
+    def pass_on(step):
+        zb, flip, block = block_at(step)
+
+        @pl.when(step == 0)
+        def _():
+            own_copy.wait()
+
+        @pl.when(step > 0)
+        def _():
+            by_width(block, lambda width: send(block, width, 0, across).wait_recv())
+
+        each_send(step, lambda copy: copy.start())
+        by_width(block, lambda width: keep(block, width).start())
+
+    def multiply(step):
+        zb, flip, block = block_at(step)
+        depth = block - 4 * core
+
+        def squares(width):
+            values = r_buf[block, :, :width].astype(jnp.float32)
+            var_out[:, :width] += jnp.sum(values * values, axis=0, keepdims=True)
+
+        by_width(block, squares)
+        for k in range(4):
+            @pl.when(depth == k)
+            def _(k=k):
+                width = widths[k]
+                r_masked[:, :width] = r_buf[block, :, :width] * mask_ref[0:1, :width].astype(jnp.bfloat16)
+
+                @pl.when(core == 0)
+                def _():
+                    @pl.loop(0, cols // CHUNK)
+                    def _(j):
+                        at = pl.ds(pl.multiple_of(j * CHUNK, CHUNK), CHUNK)
+                        p_buf[k, :, at] = jnp.dot(
+                            r_masked[:, :width], x_own[:width, at], preferred_element_type=jnp.float32
+                        ).astype(jnp.bfloat16)
+
+                @pl.when(core == 1)
+                def _():
+                    send_low(4 + k).wait_recv()
+                    low_masked[...] = r_low[k] * mask_ref[1:2, :].astype(jnp.bfloat16)
+
+                    @pl.loop(0, cols // CHUNK)
+                    def _(j):
+                        at = pl.ds(pl.multiple_of(j * CHUNK, CHUNK), CHUNK)
+                        p_buf[k, :, at] = (
+                            jnp.dot(low_masked[...], x_low[:, at], preferred_element_type=jnp.float32)
+                            + jnp.dot(r_masked[:, :width], x_own[:width, at], preferred_element_type=jnp.float32)
+                        ).astype(jnp.bfloat16)
+
+                    send_p(4 + k, k).start()
+
+                keep_p(4 * core + k, k).start()
+
+    @pl.when(core == 0)
+    def _():
+        send_x.start()
+
+    var_out[...] = jnp.zeros_like(var_out)
+    pass_on(0)
+    x_copy.wait()
+
+    @pl.when(core == 1)
+    def _():
+        send_x.wait_recv()
+
+    def turn(step, carry):
+        @pl.when(step < 8)
+        def _():
+            pass_on(step)
+
+        multiply(step - LAG)
+        return carry
+
+    lax.fori_loop(1, LAG, lambda step, carry: (pass_on(step), carry)[1], 0)
+    lax.fori_loop(LAG, 8 + LAG, turn, 0)
+
+    def finish(step, carry):
+        each_send(step, lambda copy: copy.wait_send())
+        block = block_at(step)[2]
+        by_width(block, lambda width: keep(block, width).wait())
+        return carry
+
+    lax.fori_loop(0, 8, finish, 0)
+    for k in range(4):
+        keep_p(4 * core + k, k).wait()
+
+    @pl.when(core == 0)
+    def _():
+        send_x.wait_send()
+        for k in range(4):
+            send_p(4 + k, k).wait_recv()
+
+    @pl.when(core == 1)
+    def _():
+        for k in range(4):
+            send_p(4 + k, k).wait_send()
+
+
+def gather_product(root_inv, child_off, masks):
+    rows, half = root_inv.shape
+    cols = child_off.shape[1]
+    bf16 = jnp.bfloat16
+    dma = pltpu.SemaphoreType.DMA
+    return pl.pallas_call(
+        gather_kernel,
+        out_shape=(
+            jax.ShapeDtypeStruct((8 * rows, half), bf16),
+            jax.ShapeDtypeStruct((8 * rows, cols), bf16),
+            jax.ShapeDtypeStruct((1, half), jnp.float32),
+        ),
+        in_specs=[
+            pl.BlockSpec(memory_space=pl.ANY),
+            pl.BlockSpec(memory_space=pl.ANY),
+            pl.BlockSpec(memory_space=pltpu.VMEM),
+        ],
+        out_specs=(
+            pl.BlockSpec(memory_space=pl.ANY),
+            pl.BlockSpec(memory_space=pl.ANY),
+            pl.BlockSpec(memory_space=pltpu.VMEM),
+        ),
+        scratch_shapes=[
+            pltpu.VMEM((8, rows, half), bf16),
+            pltpu.VMEM((4, rows, half), bf16),
+            pltpu.VMEM((half, cols), bf16),
+            pltpu.VMEM((half, cols), bf16),
+            pltpu.VMEM((4, rows, cols), bf16),
+            pltpu.VMEM((rows, half), bf16),
+            pltpu.VMEM((rows, half), bf16),
+            dma((8,)), dma((8, 4)), dma((4,)), dma((2,)), dma(()), dma((4,)), dma((4,)), dma((4,)), dma((8,)), dma(()),
+        ],
+        compiler_params=pltpu.CompilerParams(
+            collective_id=0, has_side_effects=True, vmem_limit_bytes=58 * 1024 * 1024
+        ),
+        cost_estimate=pl.CostEstimate(flops=36 * rows * rows * cols, bytes_accessed=60 * 2**20, transcendentals=0),
+        name="gather_product",
+    )(root_inv, child_off, masks)
+
+
+def cross_kernel(starts, flags_ref, r_ref, p_ref, off_ref, y_ref, var_ref):
+    var_ref[...] = jnp.zeros_like(var_ref)
+    total = p_ref.shape[0]
+    for t in range(len(starts)):
+        tile = slice(t * TILE, (t + 1) * TILE)
+        for core in range(2):
+            @pl.when((flags_ref[t] == 1) & (flags_ref[len(starts)] == core))
+            def _(t=t, core=core, tile=tile):
+                low = core * (total // 2) + starts[t]
+                y = -lax.dot_general(
+                    r_ref[low:, tile], p_ref[low:, :], (((0,), (0,)), ((), ())),
+                    preferred_element_type=jnp.float32,
+                )
+                y_ref[tile, :] = y
+                var_ref[...] += jnp.sum(off_ref[tile, :].astype(jnp.float32) * y, axis=0, keepdims=True)
+
+        @pl.when(flags_ref[t] == 0)
+        def _(tile=tile):
+            y_ref[tile, :] = jnp.zeros((TILE, y_ref.shape[1]), jnp.float32)
+
+
+def cross_terms(flags, root_rows, product, child_off, rows):
+    total, half = root_rows.shape
+    cols = product.shape[1]
+    widths = [min(half, -(-(k + 1) * rows // TILE) * TILE) for k in range(4)]
+    starts = [rows * next(k for k in range(4) if widths[k] > t * TILE) for t in range(half // TILE)]
+    return pl.pallas_call(
+        functools.partial(cross_kernel, starts),
+        grid_spec=pltpu.PrefetchScalarGridSpec(
+            num_scalar_prefetch=1,
+            grid=(cols // CHUNK,),
+            in_specs=[
+                pl.BlockSpec((total, half), lambda j, flags: (0, 0)),
+                pl.BlockSpec((total, CHUNK), lambda j, flags: (0, j)),
+                pl.BlockSpec((half, CHUNK), lambda j, flags: (0, j)),
+            ],
+            out_specs=[
+                pl.BlockSpec((half, CHUNK), lambda j, flags: (0, j)),
+                pl.BlockSpec((1, CHUNK), lambda j, flags: (0, j)),
+            ],
+        ),
+        out_shape=(
+            jax.ShapeDtypeStruct((half, cols), jnp.float32),
+            jax.ShapeDtypeStruct((1, cols), jnp.float32),
+        ),
+        compiler_params=pltpu.CompilerParams(vmem_limit_bytes=56 * 1024 * 1024),
+        name="cross_terms",
+    )(flags, root_rows, product, child_off)
+
+
+def fused_body(root_inv, child_off, child_inv, struct):
+    rows, half = root_inv.shape
+    cols = child_off.shape[1]
+    tiles = half // TILE
+    core = lax.axis_index("col")
+    listed = lax.dynamic_slice_in_dim(struct, lax.axis_index("row") * cols // W1, 1, axis=0)[0]
+    hits = jnp.any(jnp.arange(2 * tiles, dtype=jnp.int32)[:, None] == listed[None, :], axis=1)
+    own_hits = lax.dynamic_slice_in_dim(hits, core * tiles, tiles, axis=0)
+    masks = jnp.repeat(jnp.stack([own_hits, hits[:tiles]]).astype(jnp.float32), TILE, axis=1)
+    root_rows, product, root_var = gather_product(root_inv, child_off, masks)
+    flags = jnp.concatenate([own_hits.astype(jnp.int32), core[None].astype(jnp.int32)])
+    cross_cov, cross_var = cross_terms(flags, root_rows, product, child_off, rows)
+    local_terms = jnp.sum(jnp.square(child_inv.astype(jnp.float32)), axis=0) - cross_var[0]
+    return (cross_cov, root_var[0], lax.psum(local_terms, "col"))
+
+
+def body(row_devices, col_devices, root_inv, child_off, child_inv, struct):
+    rows, half = root_inv.shape
+    cols = child_off.shape[1]
+    fits = (
+        row_devices == 8 and col_devices == 2 and half == 4 * rows and half % TILE == 0
+        and rows % 32 == 0 and half <= 1280 and cols <= 4096 and W1 % cols == 0 and cols % CHUNK == 0
+    )
+    run = fused_body if fits else plain_body
+    return run(root_inv, child_off, child_inv, struct)
+
+
 def solution(mesh):
     placed = (
         P(("cfg", "row"), "col"),
@@ -61,7 +395,7 @@
         P("cfg", None),
     )
     return jax.shard_map(
-        body,
+        functools.partial(body, mesh.shape["row"], mesh.shape["col"]),
         mesh=mesh,
         in_specs=placed,
         out_specs=(P("col", ("cfg", "row")), P(("cfg", "col")), P(("cfg", "row"))),

time: 315 us -> 160 us (0.51)
  Pallas kernels: 0 us -> 144 us
  blocking collectives: 140 us -> 3.94 us
  matrix products: 82 us -> 0 us
  waiting for transfers between devices: 69.6 us -> 0 us
  between operations: 14.1 us -> 0.68 us
  other arithmetic: 5.58 us -> 9.43 us
    pallas_call x0 -> x2, Pallas kernels: none -> 144 us  [the longest x1 116 us: gather_product(): pl.pallas_call(gather_kernel, out_shape=(jax.ShapeDtypeStruct((8 * rows,...]
    psum x3 -> x1, blocking collectives: 140 us -> 3.94 us  [fused_body(): return (cross_cov, root_var[0], lax.psum(local_terms, 'col'))]
    dot_general x3 -> x0, matrix products: 82 us -> none  [the longest x1 41.2 us: contract_rows(): lax.dot_general(own_cols, product_rows, (((0,), (0,)), ((), ())), preferr...]
    all_gather x1 -> x0, waiting for transfers between devices: 69 us -> none  [body(): lax.all_gather(root_inv, 'row', axis=0, tiled=True)]
    reduce_sum x2 -> x1, other arithmetic: 5.45 us -> 7.27 us  [fused_body(): jnp.sum(jnp.square(child_inv.astype(jnp.float32)), axis=0) - cross_var[0]]
  transfers between devices with their start and end apart: 1 -> 0, of which waited for: 1 -> 0; matrix products, arithmetic and copies ran while one was open for 4% -> 0% of each run, Pallas kernels for 0% -> 0%
where the time goes in v1:
time: 160 us
  Pallas kernels  144 us (90%)
  other arithmetic  9.43 us (6%)
  blocking collectives  3.94 us (2%)
    pallas_call x1, Pallas kernels, gather_product(): pl.pallas_call(gather_kernel, out_shape=(jax.ShapeDtypeStruct((8 * rows,...  116 us
    pallas_call x1, Pallas kernels, cross_terms(): pl.pallas_call(functools.partial(cross_kernel, starts), grid_spec=pltpu.P...  28.6 us
    reduce_sum x1, other arithmetic, fused_body(): jnp.sum(jnp.square(child_inv.astype(jnp.float32)), axis=0) - cross_var[0]  7.27 us
    psum x1, blocking collectives, fused_body(): return (cross_cov, root_var[0], lax.psum(local_terms, 'col'))  3.94 us

profile of v1, /device:TPU:0, one launch (start us, length us, event | category | flops | bytes accessed | tf_op | source)
XLA Modules:
  0.0 159.7 jit_solution(1718624639420725818)
XLA Ops:
  0.6 0.0 copy-start
  0.7 0.7 copy-done
  1.3 0.1 fusion
  1.4 0.1 dynamic-slice_bitcast_fusion.1
  1.5 0.1 broadcast_bitcast_fusion
  1.6 0.6 copy.7
  2.2 115.7 %gather_product.1 = (bf16[2560,1280]{1,0:T(8,128)(2,1)}, bf16[2560,4096]{1,0:T(8,128)(2,1)}, f32[1,1280]{1,0:T(1,128)}) custom-call(bf16[320,1280]{1,0:T(8,128)(2,1)} %inv_ref.1, bf16[1280,4096]{1,0:T(8,128)(2,1)} %off_ref.3, f32[2,1280]{1,0:T(2,128)} %bitcast.12), custom_call_target="tpu_custom_call" | custom-call | flops 15099494400 | bytes 62914560 | tf_op jit(solution)/shard_map/gather_product/pallas_call | solution.py:278
  117.9 0.0 copy-start.1
  117.9 0.6 pad_add_fusion.flags_ref
  118.5 0.0 copy-start.2
  118.5 28.6 %cross_terms.1 = (f32[1280,4096]{1,0:T(8,128)}, f32[1,4096]{1,0:T(1,128)}) custom-call(s32[6]{0:T(128)} %pad_add_fusion.flags_ref, bf16[2560,1280]{1,0:T(8,128)(2,1)} %get-tuple-element.8.r_ref, bf16[2560,4096]{1,0:T(8,128)(2,1)} %get-tuple-element.9.p_ref, bf16[1280,4096]{1,0:T(8,128)(2,1)} %off_ref.3), custom_call_target="tpu_custom_call" | custom-call | tf_op jit(solution)/shard_map/cross_terms/pallas_call | solution.py:339
  147.1 7.3 %multiply_reduce_fusion = f32[4096]{0:T(1024)S(1)} fusion(bf16[2048,4096]{1,0:T(8,128)(2,1)} %param.6), kind=kLoop, calls=%fused_computation | loop fusion | flops 25161728 | bytes 16793600 | tf_op jit(solution)/shard_map/reduce_sum | solution.py:375
  154.4 0.7 sub.8
  155.1 3.9 %psum.7 = f32[4096]{0:T(1024)} all-reduce(f32[4096]{0:T(1024)S(1)} %sub.8), channel_id=1, replica_groups=mesh['cfg'=2,'row'=8,'col'=2] {'col'}, use_global_device_ids=true, to_apply=%region_2.3 | all-reduce | flops 4096 | bytes 32768 | tf_op jit(solution)/shard_map/psum | solution.py:376
  159.0 0.0 copy-done.2
  159.1 0.6 reduce
  159.7 0.0 copy-done.1
  (2 shorter events, 0.0 us)
Async XLA Ops:
  0.6 0.7 copy-start
  117.9 41.8 %copy-start.1 = (s32[8,5]{1,0:T(8,128)S(1)}, s32[8,5]{1,0:T(8,128)}, u32[]{:S(2)}) copy-start(s32[8,5]{1,0:T(8,128)} %param.7) | copy-start | bytes 484
  118.5 40.5 %copy-start.2 = (f32[1,1280]{1,0:T(1,128)S(1)}, f32[1,1280]{1,0:T(1,128)}, u32[]{:S(2)}) copy-start(f32[1,1280]{1,0:T(1,128)} %get-tuple-element.11) | copy-start | bytes 15364

commit v2 on v1

--- a/solution.py
+++ b/solution.py
@@ -60,15 +60,19 @@
 MESH = pl.DeviceIdType.MESH
 CHUNK = 512
 LAG = 1
+PARTS = 4
 
 
 def gather_kernel(
-    inv_ref, off_ref, mask_ref, r_out, p_out, var_out,
-    r_buf, r_low, x_own, x_low, p_buf, r_masked, low_masked,
-    recv_sem, send_sem, low_sem, x_sem, x_recv, p_send, p_recv, p_local, r_local, own_sem,
+    inv_ref, off_ref, child_ref, mask_ref, r_out, p_out, var_out, child_out,
+    r_buf, r_low, x_own, x_low, p_buf, r_masked, low_masked, child_buf, child_sum,
+    recv_sem, send_sem, low_sem, x_sem, x_recv, p_send, p_recv, p_local, r_local, own_sem, child_sem,
 ):
     rows, half = inv_ref.shape
     cols = off_ref.shape[1]
+    part = rows // PARTS
+    span = cols // PARTS
+    child_rows = child_buf.shape[1]
     row = lax.axis_index("row")
     core = lax.axis_index("col")
     z, x = row // 2, row % 2
@@ -115,17 +119,18 @@
             def _(k=k):
                 act(widths[k])
 
-    def send(block, width, way, device):
-        view = r_buf.at[block, :, pl.ds(0, width)]
+    def send(block, piece, width, way, device):
+        view = r_buf.at[block, pl.ds(piece * part, part), pl.ds(0, width)]
         return pltpu.make_async_remote_copy(
-            src_ref=view, dst_ref=view, send_sem=send_sem.at[block, way], recv_sem=recv_sem.at[block],
-            device_id=device, device_id_type=MESH,
-        )
-
-    def send_low(block):
+            src_ref=view, dst_ref=view, send_sem=send_sem.at[block * PARTS + piece, way],
+            recv_sem=recv_sem.at[block * PARTS + piece], device_id=device, device_id_type=MESH,
+        )
+
+    def send_low(block, piece):
+        at = pl.ds(piece * part, part)
         return pltpu.make_async_remote_copy(
-            src_ref=r_buf.at[block], dst_ref=r_low.at[block - 4],
-            send_sem=send_sem.at[block, 3], recv_sem=low_sem.at[block - 4],
+            src_ref=r_buf.at[block, at], dst_ref=r_low.at[block - 4, at],
+            send_sem=send_sem.at[block * PARTS + piece, 3], recv_sem=low_sem.at[(block - 4) * PARTS + piece],
             device_id={"col": 1 - core}, device_id_type=MESH,
         )
 
@@ -136,60 +141,86 @@
             r_local.at[block],
         )
 
-    def keep_p(block, slot):
+    def p_views(block, slot, piece):
+        at = pl.ds(piece * span, span)
+        return p_buf.at[slot, :, at], p_out.at[pl.ds(block * rows, rows), at]
+
+    def keep_p(block, slot, piece):
+        here, there = p_views(block, slot, piece)
+        return pltpu.make_async_copy(here, there, p_local.at[slot * PARTS + piece])
+
+    def send_p(block, slot, piece):
+        here, there = p_views(block, slot, piece)
+        return pltpu.make_async_remote_copy(
+            src_ref=here, dst_ref=there,
+            send_sem=p_send.at[slot * PARTS + piece], recv_sem=p_recv.at[slot * PARTS + piece],
+            device_id={"col": 1 - core}, device_id_type=MESH,
+        )
+
+    def child_copy(turn):
         return pltpu.make_async_copy(
-            p_buf.at[slot], p_out.at[pl.ds(block * rows, rows), :], p_local.at[slot]
-        )
-
-    def send_p(block, slot):
-        return pltpu.make_async_remote_copy(
-            src_ref=p_buf.at[slot], dst_ref=p_out.at[pl.ds(block * rows, rows), :],
-            send_sem=p_send.at[slot], recv_sem=p_recv.at[slot],
-            device_id={"col": 1 - core}, device_id_type=MESH,
-        )
-
-    def each_send(step, act):
+            child_ref.at[pl.ds(turn * child_rows, child_rows), :], child_buf.at[turn % 2], child_sem.at[turn % 2]
+        )
+
+    def child_squares(turn):
+        @pl.when(turn + 1 < 8 * PARTS)
+        def _():
+            child_copy(turn + 1).start()
+
+        child_copy(turn).wait()
+        for first in range(0, cols, CHUNK):
+            at = slice(first, first + CHUNK)
+            total = child_sum[:, at]
+            for low in range(0, child_rows, 16):
+                values = child_buf[turn % 2, low : low + 16, at].astype(jnp.float32)
+                total += values[:8] * values[:8] + values[8:] * values[8:]
+            child_sum[:, at] = total
+
+    def each_send(step, piece, act):
         zb, flip, block = block_at(step)
 
         def routes(width):
             @pl.when((flip == 0) & (zb >= z) & (z > 0))
             def _():
-                act(send(block, width, 0, below))
+                act(send(block, piece, width, 0, below))
 
             @pl.when((flip == 0) & (zb <= z) & (z < 3))
             def _():
-                act(send(block, width, 1, above))
+                act(send(block, piece, width, 1, above))
 
             @pl.when(flip == 0)
             def _():
-                act(send(block, width, 2, across))
+                act(send(block, piece, width, 2, across))
 
         by_width(block, routes)
 
         @pl.when((core == 0) & (block >= 4))
         def _():
-            act(send_low(block))
-
-    def pass_on(step):
+            act(send_low(block, piece))
+
+    def pass_on(step, piece):
         zb, flip, block = block_at(step)
 
-        @pl.when(step == 0)
+        @pl.when((step == 0) & (piece == 0))
         def _():
             own_copy.wait()
 
         @pl.when(step > 0)
         def _():
-            by_width(block, lambda width: send(block, width, 0, across).wait_recv())
-
-        each_send(step, lambda copy: copy.start())
-        by_width(block, lambda width: keep(block, width).start())
-
-    def multiply(step):
+            by_width(block, lambda width: send(block, piece, width, 0, across).wait_recv())
+
+        each_send(step, piece, lambda copy: copy.start())
+
+        @pl.when(piece == PARTS - 1)
+        def _():
+            by_width(block, lambda width: keep(block, width).start())
+
+    def multiply(step, piece):
         zb, flip, block = block_at(step)
         depth = block - 4 * core
 
         def squares(width):
-            values = r_buf[block, :, :width].astype(jnp.float32)
+            values = r_buf[block, pl.ds(piece * part, part), :width].astype(jnp.float32)
             var_out[:, :width] += jnp.sum(values * values, axis=0, keepdims=True)
 
         by_width(block, squares)
@@ -197,80 +228,110 @@
             @pl.when(depth == k)
             def _(k=k):
                 width = widths[k]
-                r_masked[:, :width] = r_buf[block, :, :width] * mask_ref[0:1, :width].astype(jnp.bfloat16)
+
+                @pl.when(piece == 0)
+                def _():
+                    r_masked[:, :width] = r_buf[block, :, :width] * mask_ref[0:1, :width].astype(jnp.bfloat16)
+
+                @pl.when((piece == 0) & (core == 1))
+                def _():
+                    for each in range(PARTS):
+                        send_low(4 + k, each).wait_recv()
+                    low_masked[...] = r_low[k] * mask_ref[1:2, :].astype(jnp.bfloat16)
 
                 @pl.when(core == 0)
                 def _():
-                    @pl.loop(0, cols // CHUNK)
+                    @pl.loop(0, span // CHUNK)
                     def _(j):
-                        at = pl.ds(pl.multiple_of(j * CHUNK, CHUNK), CHUNK)
+                        at = pl.ds(pl.multiple_of(piece * span + j * CHUNK, CHUNK), CHUNK)
                         p_buf[k, :, at] = jnp.dot(
                             r_masked[:, :width], x_own[:width, at], preferred_element_type=jnp.float32
                         ).astype(jnp.bfloat16)
 
                 @pl.when(core == 1)
                 def _():
-                    send_low(4 + k).wait_recv()
-                    low_masked[...] = r_low[k] * mask_ref[1:2, :].astype(jnp.bfloat16)
-
-                    @pl.loop(0, cols // CHUNK)
+                    @pl.loop(0, span // CHUNK)
                     def _(j):
-                        at = pl.ds(pl.multiple_of(j * CHUNK, CHUNK), CHUNK)
+                        at = pl.ds(pl.multiple_of(piece * span + j * CHUNK, CHUNK), CHUNK)
                         p_buf[k, :, at] = (
                             jnp.dot(low_masked[...], x_low[:, at], preferred_element_type=jnp.float32)
                             + jnp.dot(r_masked[:, :width], x_own[:width, at], preferred_element_type=jnp.float32)
                         ).astype(jnp.bfloat16)
 
-                    send_p(4 + k, k).start()
-
-                keep_p(4 * core + k, k).start()
+                    send_p(4 + k, k, piece).start()
+
+                keep_p(4 * core + k, k, piece).start()
+
+    child_copy(0).start()
 
     @pl.when(core == 0)
     def _():
         send_x.start()
 
     var_out[...] = jnp.zeros_like(var_out)
-    pass_on(0)
-    x_copy.wait()
-
-    @pl.when(core == 1)
-    def _():
-        send_x.wait_recv()
-
-    def turn(step, carry):
-        @pl.when(step < 8)
-        def _():
-            pass_on(step)
-
-        multiply(step - LAG)
+    child_sum[...] = jnp.zeros_like(child_sum)
+    first_low = 2 * (2 - z) * (1 - z // 2)
+
+    def turn(n, carry):
+        step, piece = n // PARTS, n % PARTS
+
+        @pl.when(n < 8 * PARTS)
+        def _():
+            pass_on(step, piece)
+            child_squares(n)
+
+        @pl.when(n == LAG * PARTS)
+        def _():
+            x_copy.wait()
+
+        @pl.when((core == 1) & (n == (first_low + LAG) * PARTS))
+        def _():
+            send_x.wait_recv()
+
+        @pl.when(n >= LAG * PARTS)
+        def _():
+            multiply(step - LAG, piece)
+
         return carry
 
-    lax.fori_loop(1, LAG, lambda step, carry: (pass_on(step), carry)[1], 0)
-    lax.fori_loop(LAG, 8 + LAG, turn, 0)
-
-    def finish(step, carry):
-        each_send(step, lambda copy: copy.wait_send())
+    lax.fori_loop(0, (8 + LAG) * PARTS, turn, 0)
+    child_out[...] = jnp.sum(child_sum[...], axis=0, keepdims=True)
+
+    def finish(n, carry):
+        each_send(n // PARTS, n % PARTS, lambda copy: copy.wait_send())
+        return carry
+
+    lax.fori_loop(0, 8 * PARTS, finish, 0)
+
+    def kept(step, carry):
         block = block_at(step)[2]
         by_width(block, lambda width: keep(block, width).wait())
         return carry
 
-    lax.fori_loop(0, 8, finish, 0)
-    for k in range(4):
-        keep_p(4 * core + k, k).wait()
+    lax.fori_loop(0, 8, kept, 0)
+
+    def product_done(n, carry):
+        slot, piece = n // PARTS, n % PARTS
+        keep_p(4 * core + slot, slot, piece).wait()
+
+        @pl.when(core == 0)
+        def _():
+            send_p(4 + slot, slot, piece).wait_recv()
+
+        @pl.when(core == 1)
+        def _():
+            send_p(4 + slot, slot, piece).wait_send()
+
+        return carry
+
+    lax.fori_loop(0, 4 * PARTS, product_done, 0)
 
     @pl.when(core == 0)
     def _():
         send_x.wait_send()
-        for k in range(4):
-            send_p(4 + k, k).wait_recv()
-
-    @pl.when(core == 1)
-    def _():
-        for k in range(4):
-            send_p(4 + k, k).wait_send()
-
-
-def gather_product(root_inv, child_off, masks):
+
+
+def gather_product(root_inv, child_off, child_inv, masks):
     rows, half = root_inv.shape
     cols = child_off.shape[1]
     bf16 = jnp.bfloat16
@@ -281,8 +342,10 @@
             jax.ShapeDtypeStruct((8 * rows, half), bf16),
             jax.ShapeDtypeStruct((8 * rows, cols), bf16),
             jax.ShapeDtypeStruct((1, half), jnp.float32),
+            jax.ShapeDtypeStruct((1, cols), jnp.float32),
         ),
         in_specs=[
+            pl.BlockSpec(memory_space=pl.ANY),
             pl.BlockSpec(memory_space=pl.ANY),
             pl.BlockSpec(memory_space=pl.ANY),
             pl.BlockSpec(memory_space=pltpu.VMEM),
@@ -290,6 +353,7 @@
         out_specs=(
             pl.BlockSpec(memory_space=pl.ANY),
             pl.BlockSpec(memory_space=pl.ANY),
+            pl.BlockSpec(memory_space=pltpu.VMEM),
             pl.BlockSpec(memory_space=pltpu.VMEM),
         ),
         scratch_shapes=[
@@ -300,14 +364,17 @@
             pltpu.VMEM((4, rows, cols), bf16),
             pltpu.VMEM((rows, half), bf16),
             pltpu.VMEM((rows, half), bf16),
-            dma((8,)), dma((8, 4)), dma((4,)), dma((2,)), dma(()), dma((4,)), dma((4,)), dma((4,)), dma((8,)), dma(()),
+            pltpu.VMEM((2, child_inv.shape[0] // (8 * PARTS), cols), bf16),
+            pltpu.VMEM((8, cols), jnp.float32),
+            dma((8 * PARTS,)), dma((8 * PARTS, 4)), dma((4 * PARTS,)), dma((2,)), dma(()),
+            dma((4 * PARTS,)), dma((4 * PARTS,)), dma((4 * PARTS,)), dma((8,)), dma(()), dma((2,)),
         ],
         compiler_params=pltpu.CompilerParams(
             collective_id=0, has_side_effects=True, vmem_limit_bytes=58 * 1024 * 1024
         ),
         cost_estimate=pl.CostEstimate(flops=36 * rows * rows * cols, bytes_accessed=60 * 2**20, transcendentals=0),
         name="gather_product",
-    )(root_inv, child_off, masks)
+    )(root_inv, child_off, child_inv, masks)
 
 
 def cross_kernel(starts, flags_ref, r_ref, p_ref, off_ref, y_ref, var_ref):
@@ -369,10 +436,10 @@
     hits = jnp.any(jnp.arange(2 * tiles, dtype=jnp.int32)[:, None] == listed[None, :], axis=1)
     own_hits = lax.dynamic_slice_in_dim(hits, core * tiles, tiles, axis=0)
     masks = jnp.repeat(jnp.stack([own_hits, hits[:tiles]]).astype(jnp.float32), TILE, axis=1)
-    root_rows, product, root_var = gather_product(root_inv, child_off, masks)
+    root_rows, product, root_var, child_squares = gather_product(root_inv, child_off, child_inv, masks)
     flags = jnp.concatenate([own_hits.astype(jnp.int32), core[None].astype(jnp.int32)])
     cross_cov, cross_var = cross_terms(flags, root_rows, product, child_off, rows)
-    local_terms = jnp.sum(jnp.square(child_inv.astype(jnp.float32)), axis=0) - cross_var[0]
+    local_terms = child_squares[0] - cross_var[0]
     return (cross_cov, root_var[0], lax.psum(local_terms, "col"))
 
 
@@ -381,7 +448,7 @@
     cols = child_off.shape[1]
     fits = (
         row_devices == 8 and col_devices == 2 and half == 4 * rows and half % TILE == 0
-        and rows % 32 == 0 and half <= 1280 and cols <= 4096 and W1 % cols == 0 and cols % CHUNK == 0
+        and rows % 64 == 0 and child_inv.shape[0] % 512 == 0 and half <= 1280 and cols <= 4096 and W1 % cols == 0 and cols % (PARTS * CHUNK) == 0
     )
     run = fused_body if fits else plain_body
     return run(root_inv, child_off, child_inv, struct)

time: 160 us -> 125 us (0.78)
  Pallas kernels: 144 us -> 118 us
  other arithmetic: 9.43 us -> 2.17 us
    pallas_call x1, Pallas kernels: 116 us -> 85.1 us  [gather_product(): pl.pallas_call(gather_kernel, out_shape=(jax.ShapeDtypeStruct((8 * rows,...]
    reduce_sum x1 -> x0, other arithmetic: 7.27 us -> none  [fused_body(): jnp.sum(jnp.square(child_inv.astype(jnp.float32)), axis=0) - cross_var[0]]
    pallas_call x1, Pallas kernels: 28.6 us -> 32.5 us  [cross_terms(): pl.pallas_call(functools.partial(cross_kernel, starts), grid_spec=pltpu.P...]
where the time goes in v2:
time: 125 us; the launch traced here: 126 us
  Pallas kernels  118 us (94%)
  blocking collectives  3.96 us (3%)
  other arithmetic  2.17 us (2%)
  local copies, waits for them, and re-layouts  1.37 us (1%)
    pallas_call x1, Pallas kernels, gather_product(): pl.pallas_call(gather_kernel, out_shape=(jax.ShapeDtypeStruct((8 * rows,...  85.1 us
    pallas_call x1, Pallas kernels, cross_terms(): pl.pallas_call(functools.partial(cross_kernel, starts), grid_spec=pltpu.P...  32.5 us
    psum x1, blocking collectives, fused_body(): return (cross_cov, root_var[0], lax.psum(local_terms, 'col'))  3.96 us

profile of v2, /device:TPU:0, one launch (start us, length us, event | category | flops | bytes accessed | tf_op | source)
XLA Modules:
  0.0 125.8 jit_solution(5546740546882167207)
XLA Ops:
  0.6 0.0 copy-start
  0.7 0.7 copy-done
  1.3 0.1 fusion
  1.4 0.1 dynamic-slice_bitcast_fusion.1
  1.5 0.6 pad_add_fusion.flags_ref
  2.2 0.1 broadcast_bitcast_fusion
  2.2 0.6 copy.7
  2.8 85.1 %gather_product.1 = (bf16[2560,1280]{1,0:T(8,128)(2,1)}, bf16[2560,4096]{1,0:T(8,128)(2,1)}, f32[1,1280]{1,0:T(1,128)}, f32[1,4096]{1,0:T(1,128)}) custom-call(bf16[320,1280]{1,0:T(8,128)(2,1)} %inv_ref.1, bf16[1280,4096]{1,0:T(8,128)(2,1)} %off_ref.3, bf16[2048,4096]{1,0:T(8,128)(2,1)} %child_ref.1, f32[2,1280]{1,0:T(2,128)} %bitcast.12), custom_call_target="tpu_custom_call" | custom-call | flops 15099494400 | bytes 62914560 | tf_op jit(solution)/shard_map/gather_product/pallas_call | solution.py:339
  87.9 0.0 copy-start.1
  88.0 0.0 copy-start.2
  88.0 0.0 copy-start.3
  88.0 32.5 %cross_terms.1 = (f32[1280,4096]{1,0:T(8,128)}, f32[1,4096]{1,0:T(1,128)}) custom-call(s32[6]{0:T(128)} %pad_add_fusion.flags_ref, bf16[2560,1280]{1,0:T(8,128)(2,1)} %get-tuple-element.9.r_ref, bf16[2560,4096]{1,0:T(8,128)(2,1)} %get-tuple-element.10.p_ref, bf16[1280,4096]{1,0:T(8,128)(2,1)} %off_ref.3), custom_call_target="tpu_custom_call" | custom-call | tf_op jit(solution)/shard_map/cross_terms/pallas_call | solution.py:406
  120.5 0.0 copy-done.2
  120.5 0.7 sub.11
  121.2 4.0 %psum.7 = f32[4096]{0:T(1024)} all-reduce(f32[4096]{0:T(1024)S(1)} %bitcast.11), channel_id=1, replica_groups=mesh['cfg'=2,'row'=8,'col'=2] {'col'}, use_global_device_ids=true, to_apply=%region_1.2 | all-reduce | flops 4096 | bytes 32768 | tf_op jit(solution)/shard_map/psum | solution.py:443
  125.2 0.0 copy-done.3
  125.2 0.6 reduce
  125.8 0.0 copy-done.1
  (2 shorter events, 0.0 us)
Async XLA Ops:
  0.6 0.7 copy-start
  87.9 37.9 %copy-start.1 = (s32[8,5]{1,0:T(8,128)S(1)}, s32[8,5]{1,0:T(8,128)}, u32[]{:S(2)}) copy-start(s32[8,5]{1,0:T(8,128)} %param.7) | copy-start | bytes 484
  88.0 32.6 %copy-start.2 = (f32[1,4096]{1,0:T(1,128)S(1)}, f32[1,4096]{1,0:T(1,128)}, u32[]{:S(2)}) copy-start(f32[1,4096]{1,0:T(1,128)} %get-tuple-element.13) | copy-start | bytes 49156
  88.0 37.2 %copy-start.3 = (f32[1,1280]{1,0:T(1,128)S(1)}, f32[1,1280]{1,0:T(1,128)}, u32[]{:S(2)}) copy-start(f32[1,1280]{1,0:T(1,128)} %get-tuple-element.12) | copy-start | bytes 15364

commit v3 on v2

--- a/solution.py
+++ b/solution.py
@@ -59,8 +59,9 @@
 
 MESH = pl.DeviceIdType.MESH
 CHUNK = 512
-LAG = 1
 PARTS = 4
+LAG = 3
+BLOCK = 1024
 
 
 def gather_kernel(
@@ -280,21 +281,21 @@
             pass_on(step, piece)
             child_squares(n)
 
-        @pl.when(n == LAG * PARTS)
+        @pl.when(n == LAG)
         def _():
             x_copy.wait()
 
-        @pl.when((core == 1) & (n == (first_low + LAG) * PARTS))
+        @pl.when((core == 1) & (n == first_low * PARTS + LAG))
         def _():
             send_x.wait_recv()
 
-        @pl.when(n >= LAG * PARTS)
-        def _():
-            multiply(step - LAG, piece)
+        @pl.when(n >= LAG)
+        def _():
+            multiply((n - LAG) // PARTS, (n - LAG) % PARTS)
 
         return carry
 
-    lax.fori_loop(0, (8 + LAG) * PARTS, turn, 0)
+    lax.fori_loop(0, 8 * PARTS + LAG, turn, 0)
     child_out[...] = jnp.sum(child_sum[...], axis=0, keepdims=True)
 
     def finish(n, carry):
@@ -377,7 +378,14 @@
     )(root_inv, child_off, child_inv, masks)
 
 
-def cross_kernel(starts, flags_ref, r_ref, p_ref, off_ref, y_ref, var_ref):
+def cross_kernel(starts, flags_ref, r_ref, p_ref, off_ref, y_ref, var_ref, turned):
+    @pl.when(pl.program_id(0) == 0)
+    def _():
+        for t in range(len(starts)):
+            @pl.when(flags_ref[t] == 1)
+            def _(t=t):
+                turned[t * TILE : (t + 1) * TILE, :] = r_ref[:, t * TILE : (t + 1) * TILE].T
+
     var_ref[...] = jnp.zeros_like(var_ref)
     total = p_ref.shape[0]
     for t in range(len(starts)):
@@ -386,10 +394,7 @@
             @pl.when((flags_ref[t] == 1) & (flags_ref[len(starts)] == core))
             def _(t=t, core=core, tile=tile):
                 low = core * (total // 2) + starts[t]
-                y = -lax.dot_general(
-                    r_ref[low:, tile], p_ref[low:, :], (((0,), (0,)), ((), ())),
-                    preferred_element_type=jnp.float32,
-                )
+                y = -jnp.dot(turned[tile, low:], p_ref[low:, :], preferred_element_type=jnp.float32)
                 y_ref[tile, :] = y
                 var_ref[...] += jnp.sum(off_ref[tile, :].astype(jnp.float32) * y, axis=0, keepdims=True)
 
@@ -407,16 +412,17 @@
         functools.partial(cross_kernel, starts),
         grid_spec=pltpu.PrefetchScalarGridSpec(
             num_scalar_prefetch=1,
-            grid=(cols // CHUNK,),
+            grid=(cols // BLOCK,),
             in_specs=[
-                pl.BlockSpec((total, half), lambda j, flags: (0, 0)),
-                pl.BlockSpec((total, CHUNK), lambda j, flags: (0, j)),
-                pl.BlockSpec((half, CHUNK), lambda j, flags: (0, j)),
+                pl.BlockSpec((total, half), lambda j, flags: (0, 0), pipeline_mode=pl.Buffered(1)),
+                pl.BlockSpec((total, BLOCK), lambda j, flags: (0, j)),
+                pl.BlockSpec((half, BLOCK), lambda j, flags: (0, j)),
             ],
             out_specs=[
-                pl.BlockSpec((half, CHUNK), lambda j, flags: (0, j)),
-                pl.BlockSpec((1, CHUNK), lambda j, flags: (0, j)),
+                pl.BlockSpec((half, BLOCK), lambda j, flags: (0, j)),
+                pl.BlockSpec((1, BLOCK), lambda j, flags: (0, j)),
             ],
+            scratch_shapes=[pltpu.VMEM((half, total), jnp.bfloat16)],
         ),
         out_shape=(
             jax.ShapeDtypeStruct((half, cols), jnp.float32),
@@ -448,7 +454,7 @@
     cols = child_off.shape[1]
     fits = (
         row_devices == 8 and col_devices == 2 and half == 4 * rows and half % TILE == 0
-        and rows % 64 == 0 and child_inv.shape[0] % 512 == 0 and half <= 1280 and cols <= 4096 and W1 % cols == 0 and cols % (PARTS * CHUNK) == 0
+        and rows % 64 == 0 and child_inv.shape[0] % 512 == 0 and half <= 1280 and cols <= 4096 and W1 % cols == 0 and cols % (PARTS * CHUNK) == 0 and cols % BLOCK == 0
     )
     run = fused_body if fits else plain_body
     return run(root_inv, child_off, child_inv, struct)

time: 125 us -> 125 us (level)
  the two profiles are of different devices: /device:TPU:0 before, /device:TPU:3 now
where the time goes in v3:
time: 125 us; the launch traced here: 126 us
  Pallas kernels  104 us (83%)
  blocking collectives  17 us (14%)
  other arithmetic  2.17 us (2%)
  local copies, waits for them, and re-layouts  1.37 us (1%)
    pallas_call x1, Pallas kernels, gather_product(): pl.pallas_call(gather_kernel, out_shape=(jax.ShapeDtypeStruct((8 * rows,...  84.1 us
    pallas_call x1, Pallas kernels, cross_terms(): pl.pallas_call(functools.partial(cross_kernel, starts), grid_spec=pltpu.P...  20.3 us
    psum x1, blocking collectives, fused_body(): return (cross_cov, root_var[0], lax.psum(local_terms, 'col'))  17 us

profile of v3, /device:TPU:3, one launch (start us, length us, event | category | flops | bytes accessed | tf_op | source)
XLA Modules:
  0.0 125.6 jit_solution(1336926222771321834)
XLA Ops:
  0.6 0.0 copy-start
  0.7 0.7 copy-done
  1.3 0.1 fusion
  1.4 0.1 dynamic-slice_bitcast_fusion.1
  1.5 0.6 pad_add_fusion.flags_ref
  2.2 0.1 broadcast_bitcast_fusion
  2.2 0.6 copy.7
  2.8 84.1 %gather_product.1 = (bf16[2560,1280]{1,0:T(8,128)(2,1)}, bf16[2560,4096]{1,0:T(8,128)(2,1)}, f32[1,1280]{1,0:T(1,128)}, f32[1,4096]{1,0:T(1,128)}) custom-call(bf16[320,1280]{1,0:T(8,128)(2,1)} %inv_ref.1, bf16[1280,4096]{1,0:T(8,128)(2,1)} %off_ref.3, bf16[2048,4096]{1,0:T(8,128)(2,1)} %child_ref.1, f32[2,1280]{1,0:T(2,128)} %bitcast.12), custom_call_target="tpu_custom_call" | custom-call | flops 15099494400 | bytes 62914560 | tf_op jit(solution)/shard_map/gather_product/pallas_call | solution.py:340
  86.9 0.0 copy-start.1
  87.0 0.0 copy-start.2
  87.0 0.0 copy-start.3
  87.0 20.3 %cross_terms.1 = (f32[1280,4096]{1,0:T(8,128)}, f32[1,4096]{1,0:T(1,128)}) custom-call(s32[6]{0:T(128)} %pad_add_fusion.flags_ref, bf16[2560,1280]{1,0:T(8,128)(2,1)} %get-tuple-element.9.r_ref, bf16[2560,4096]{1,0:T(8,128)(2,1)} %get-tuple-element.10.p_ref, bf16[1280,4096]{1,0:T(8,128)(2,1)} %off_ref.3), custom_call_target="tpu_custom_call" | custom-call | tf_op jit(solution)/shard_map/cross_terms/pallas_call | solution.py:411
  107.3 0.0 copy-done.2
  107.3 0.7 sub.11
  108.0 17.0 %psum.7 = f32[4096]{0:T(1024)} all-reduce(f32[4096]{0:T(1024)S(1)} %bitcast.11), channel_id=1, replica_groups=mesh['cfg'=2,'row'=8,'col'=2] {'col'}, use_global_device_ids=true, to_apply=%region_1.2 | all-reduce | flops 4096 | bytes 32768 | tf_op jit(solution)/shard_map/psum | solution.py:449
  125.0 0.0 copy-done.3
  125.0 0.6 reduce
  125.6 0.0 copy-done.1
  (2 shorter events, 0.0 us)
Async XLA Ops:
  0.6 0.7 copy-start
  86.9 38.7 %copy-start.1 = (s32[8,5]{1,0:T(8,128)S(1)}, s32[8,5]{1,0:T(8,128)}, u32[]{:S(2)}) copy-start(s32[8,5]{1,0:T(8,128)} %param.7) | copy-start | bytes 484
  87.0 20.3 %copy-start.2 = (f32[1,4096]{1,0:T(1,128)S(1)}, f32[1,4096]{1,0:T(1,128)}, u32[]{:S(2)}) copy-start(f32[1,4096]{1,0:T(1,128)} %get-tuple-element.13) | copy-start | bytes 49156
  87.0 38.0 %copy-start.3 = (f32[1,1280]{1,0:T(1,128)S(1)}, f32[1,1280]{1,0:T(1,128)}, u32[]{:S(2)}) copy-start(f32[1,1280]{1,0:T(1,128)} %get-tuple-element.12) | copy-start | bytes 15364
